TPU v7x, 32 devices: a whole 2x2x4 slice. The times are simulated.
32 devices in a mesh: section: 4 (over y, x), dp: 8 (over z, core).
Axes of the slice: x: 2, y: 2, z: 4, core: 2. Of those that a mesh axis runs over, the one named last changes fastest.
Arguments:
- frames: bfloat16 [2, 512, 4096], P(None, 'dp'), may hold values from -6 to 6
- grad_out: bfloat16 [2, 512, 4096], P(None, 'dp'), may hold values from -6 to 6
- norm_gain: bfloat16 [4, 4096], P('section', 'dp'), may hold values from 0.5 to 1.5
- w_reduce: bfloat16 [4, 4096, 512], P('section', 'dp'), may hold values from -0.09375 to 0.09375
- w_restore: bfloat16 [4, 512, 4096], P('section', None, 'dp'), may hold values from -0.25 to 0.25
Outputs:
- grad_gain: float32 [4, 4096], P('section', 'dp')
- grad_reduce: float32 [4, 4096, 512], P('section', 'dp')
- grad_restore: float32 [4, 512, 4096], P('section', None, 'dp')
All inputs are finite; a program needn't handle non-finite values.
Results may differ from a plain program's by a relative error of at most 0.023.
Values may be sent and summed in bfloat16 or wider, within the bound.
A program may use at most 128 MiB of HBM per device.

v0:
```python
import jax
import jax.numpy as jnp
from jax import lax
from jax.sharding import PartitionSpec as P

POOL = 4


epsilon = 1e-06


def from_partner(block, axis, distance):
    count = lax.axis_size(axis)
    route = []
    for low in range(count):
        high = low | 1 << distance
        if high != low and high < count:
            route += [(low, high), (high, low)]
    return lax.ppermute(block, axis, route)


def from_behind(block, axis, distance):
    devices = range(lax.axis_size(axis))
    route = [(i - distance, i) for i in devices if i - distance in devices]
    return lax.ppermute(block, axis, route)


def normalize(inputs, gain_row):
    values = inputs.astype(jnp.float32)
    inverse = lax.rsqrt(jnp.mean(values * values, axis=-1, keepdims=True) + epsilon)
    normal = values * inverse
    return (values, inverse, normal, (normal * gain_row.astype(jnp.float32)).astype(jnp.bfloat16))


def section_forward(inputs, gain_row, matrix_reduce, matrix_restore):
    values, inverse, normal, normed = normalize(inputs, gain_row)
    before = jnp.dot(normed, matrix_reduce, preferred_element_type=jnp.float32)
    active = (before * jax.nn.sigmoid(before)).astype(jnp.bfloat16)
    return (values + jnp.dot(active, matrix_restore, preferred_element_type=jnp.float32)).astype(
        jnp.bfloat16
    )


def section_backward(inputs, upstream, gain_row, matrix_reduce, matrix_restore):
    values, inverse, normal, normed = normalize(inputs, gain_row)
    before = jnp.dot(normed, matrix_reduce, preferred_element_type=jnp.float32)
    gating = jax.nn.sigmoid(before)
    active = (before * gating).astype(jnp.bfloat16)
    grad_active = lax.dot_general(
        upstream, matrix_restore, (((1,), (1,)), ((), ())), preferred_element_type=jnp.float32
    )
    grad_before = (grad_active * gating * (1.0 + before * (1.0 - gating))).astype(jnp.bfloat16)
    grad_normed = lax.dot_general(
        grad_before, matrix_reduce, (((1,), (1,)), ((), ())), preferred_element_type=jnp.float32
    )
    gain_term = jnp.sum(grad_normed * normal, axis=0)
    grad_normal = grad_normed * gain_row.astype(jnp.float32)
    projected = jnp.mean(grad_normal * normal, axis=-1, keepdims=True)
    grad_inputs = (
        upstream.astype(jnp.float32) + inverse * (grad_normal - normal * projected)
    ).astype(jnp.bfloat16)
    return (grad_inputs, normed, grad_before, active, gain_term)


def smooth_rows(block):
    values = block.astype(jnp.float32)
    grouped = values.reshape(values.shape[0] // POOL, POOL, values.shape[1])
    group_means = jnp.mean(grouped, axis=1, keepdims=True)
    return jnp.broadcast_to(group_means, grouped.shape).reshape(values.shape)


def mirror(stacked, sections):
    carried = stacked
    for bit_number in range(sections.bit_length() - 1):
        carried = from_partner(carried, "section", bit_number)
    return carried


def body(frames, grad_out, norm_gain, w_reduce, w_restore):
    sections = lax.axis_size("section")
    middle = sections // 2
    position_here = lax.axis_index("section")
    batches = frames.shape[0]
    features = frames.shape[2]
    latent = w_reduce.shape[2]
    gathered = (
        lax.all_gather(norm_gain, "dp", axis=1, tiled=True),
        lax.all_gather(w_reduce, "dp", axis=1, tiled=True),
        lax.all_gather(w_restore, "dp", axis=2, tiled=True),
    )
    gain_row = gathered[0][0]
    matrix_reduce = gathered[1][0]
    matrix_restore = gathered[2][0]
    is_down = position_here < middle
    is_up = jnp.logical_not(is_down)
    rounds = middle + batches - 1
    zeroed = jnp.zeros_like(frames)
    starting_none = jnp.zeros(frames.shape, jnp.float32)
    never = position_here < 0

    def incoming_rows(head, pooled, starting, received, chosen):
        arrived = received.astype(jnp.float32)
        arrived = jnp.where(pooled, smooth_rows(received) + arrived, arrived)
        return jnp.where(head, starting[chosen], arrived)

    def forward_sweep(
        starting, beside, offset, working, head, pooled, count, inputs_kept, outputs_kept
    ):

        def forward_advance(moment, status):
            received, inputs_kept, outputs_kept = status
            current = moment - offset
            usable = working & (current >= 0) & (current < batches)
            chosen = jnp.clip(current, 0, batches - 1)
            incoming = incoming_rows(head, pooled, starting, received, chosen)
            side = jnp.where(pooled, 0.0, beside[chosen].astype(jnp.float32))
            inputs = (incoming + side).astype(jnp.bfloat16)
            output = section_forward(inputs, gain_row, matrix_reduce, matrix_restore)
            sending = jnp.where(working, output, outputs_kept[chosen])
            inputs_kept = inputs_kept.at[chosen].set(jnp.where(usable, inputs, inputs_kept[chosen]))
            outputs_kept = outputs_kept.at[chosen].set(
                jnp.where(usable, output, outputs_kept[chosen])
            )
            received = from_behind(sending, "section", 1)
            return (received, inputs_kept, outputs_kept)

        initial = (jnp.zeros_like(frames[0]), inputs_kept, outputs_kept)
        finished = lax.fori_loop(0, count, forward_advance, initial)
        return (finished[1], finished[2])

    inputs_kept, outputs_kept = forward_sweep(
        frames.astype(jnp.float32),
        zeroed,
        position_here,
        is_down,
        position_here == 0,
        never,
        rounds,
        zeroed,
        zeroed,
    )
    mirrored = mirror(outputs_kept, sections)
    inputs_kept, outputs_kept = forward_sweep(
        starting_none,
        mirrored,
        position_here - middle + 1,
        is_up,
        never,
        position_here == middle,
        rounds + 1,
        inputs_kept,
        outputs_kept,
    )

    def backward_sweep(starting, beside, offset, working, head, pooled, count, status_in):

        def backward_advance(moment, status):
            received, returned, saved_rows, totals = status
            current = moment - offset
            usable = working & (current >= 0) & (current < batches)
            chosen = jnp.clip(current, 0, batches - 1)
            incoming = incoming_rows(head, pooled, starting, received, chosen)
            side = jnp.where(pooled, 0.0, beside[chosen].astype(jnp.float32))
            upstream = (incoming + side).astype(jnp.bfloat16)
            grad_inputs, normed, grad_before, active, gain_term = section_backward(
                inputs_kept[chosen], upstream, gain_row, matrix_reduce, matrix_restore
            )
            sending = jnp.where(working, grad_inputs, returned[chosen])
            returned = returned.at[chosen].set(jnp.where(usable, grad_inputs, returned[chosen]))
            gain_total = totals[0] + jnp.where(usable, gain_term, 0.0)
            fresh_rows = (normed, grad_before, active, upstream)
            saved_rows = tuple(
                (
                    kept_array.at[chosen].set(jnp.where(usable, fresh_item, kept_array[chosen]))
                    for kept_array, fresh_item in zip(saved_rows, fresh_rows)
                )
            )
            totals = (gain_total,)
            received = from_behind(sending, "section", -1)
            return (received, returned, saved_rows, totals)

        initial = (jnp.zeros_like(frames[0]),) + status_in
        finished = lax.fori_loop(0, count, backward_advance, initial)
        return (finished[1], finished[2], finished[3])

    gain_zero = jnp.zeros((features,), jnp.float32)
    branch_zero = jnp.zeros((batches, frames.shape[1], latent), jnp.bfloat16)
    saved_rows = (zeroed, branch_zero, branch_zero, zeroed)
    totals = (gain_zero,)
    returned, saved_rows, totals = backward_sweep(
        grad_out.astype(jnp.float32),
        zeroed,
        sections - 1 - position_here,
        is_up,
        position_here == sections - 1,
        never,
        rounds,
        (zeroed, saved_rows, totals),
    )
    mirrored_back = mirror(returned, sections)
    returned, saved_rows, totals = backward_sweep(
        starting_none,
        mirrored_back,
        middle - position_here,
        is_down,
        never,
        position_here == middle - 1,
        rounds + 1,
        (returned, saved_rows, totals),
    )
    grad_gain = lax.psum_scatter(totals[0], "dp", scatter_dimension=0, tiled=True)
    normed_all = saved_rows[0].reshape(-1, features)
    before_all = saved_rows[1].reshape(-1, latent)
    active_all = saved_rows[2].reshape(-1, latent)
    upstream_all = saved_rows[3].reshape(-1, features)
    shard_rows = before_all.shape[0]
    column_normed, column_upstream = (
        lax.all_to_all(normed_all, "dp", split_axis=1, concat_axis=0, tiled=True),
        lax.all_to_all(upstream_all, "dp", split_axis=1, concat_axis=0, tiled=True),
    )
    shard_width = column_normed.shape[1]
    pieces = (
        lax.all_gather(before_all, "dp", axis=0, tiled=True),
        lax.all_gather(active_all, "dp", axis=0, tiled=True),
    )
    length = pieces[0].shape[0]
    count = length // shard_rows
    left_rows = column_normed.reshape(count, shard_rows, shard_width)
    right_rows = column_upstream.reshape(count, shard_rows, shard_width)
    before_rows = pieces[0].reshape(count, shard_rows, latent)
    active_rows = pieces[1].reshape(count, shard_rows, latent)
    terms_reduce = jnp.einsum(
        "knd,knr->kdr", left_rows, before_rows, preferred_element_type=jnp.float32
    )
    terms_restore = jnp.einsum(
        "knr,knd->krd", active_rows, right_rows, preferred_element_type=jnp.float32
    )
    grad_reduce = jnp.sum(terms_reduce.astype(jnp.bfloat16).astype(jnp.float32), axis=0)
    grad_restore = jnp.sum(terms_restore.astype(jnp.bfloat16).astype(jnp.float32), axis=0)
    return (grad_gain[None], grad_reduce[None], grad_restore[None])


def solution(mesh):
    in_specs = (
        P(None, "dp", None),
        P(None, "dp", None),
        P("section", "dp"),
        P("section", "dp", None),
        P("section", None, "dp"),
    )
    out_specs = (P("section", "dp"), P("section", "dp", None), P("section", None, "dp"))
    return jax.shard_map(body, mesh=mesh, in_specs=in_specs, out_specs=out_specs, check_vma=False)
```

profile of v0, /device:TPU:0, one launch (start us, length us, event | category | flops | bytes accessed | tf_op | source)
XLA Modules:
  0.0 687.6 jit_solution(10406558014732686973)
XLA Ops:
  8.7 14.5 %all_gather.15 = bf16[1,4096]{1,0:T(2,128)(2,1)S(1)} all-gather(bf16[1,512]{1,0:T(2,128)(2,1)} %param.43), channel_id=1, replica_groups=mesh['section'=4,'dp'=8] {'dp'}, dimensions={1}, use_global_device_ids=true | all-gather | bytes 9216 | tf_op jit(solution)/shard_map/all_gather | solution.py:87
  23.2 36.2 %all-gather.5.cloned.1.call-done = bf16[1,4096,512]{2,1,0:T(8,128)(2,1)} async-done(((bf16[1,512,512]{2,1,0:T(8,128)(2,1)}), bf16[1,4096,512]{2,1,0:T(8,128)(2,1)}) %all-gather.5.cloned.1.call-update) | async-done | bytes 4194320 | tf_op jit(solution)/shard_map/all_gather | solution.py:88
  59.5 47.5 %all-gather.7.cloned.1.call-done = bf16[1,512,4096]{2,1,0:T(8,128)(2,1)} async-done(((bf16[1,512,512]{2,1,0:T(8,128)(2,1)}), bf16[1,512,4096]{2,1,0:T(8,128)(2,1)}) %all-gather.7.cloned.1.call-update) | async-done | bytes 4194320 | tf_op jit(solution)/shard_map/all_gather | solution.py:89
  108.2 78.1 %while.99 = (s32[]{:T(128)}, bf16[64,4096]{1,0:T(8,128)(2,1)S(1)}, bf16[2,64,4096]{2,1,0:T(8,128)(2,1)S(1)}, bf16[2,64,4096]{2,1,0:T(8,128)(2,1)}, pred[]{:T(512...) while((s32[]{:T(128)}, bf16[64,4096]{1,0:T(8,128)(2,1)S(1)}, ...), condition=%wide.region_4.5_spmd, body=%wide.region_0.4_spmd.sunk | while | flops 542281792 | bytes 33597876 | solution.py:128
  113.1 5.3 fusion.167
  124.2 10.3 %collective-permute-done = bf16[64,4096]{1,0:T(8,128)(2,1)S(1)} collective-permute-done((bf16[64,4096]{1,0:T(8,128)(2,1)}, bf16[64,4096]{1,0:T(8,128)(2,1)S(1)}, u32[]{:S(2)}, u32[]{:S(2)}) %collective-permute-start) | collective-permute-done | bytes 524320 | tf_op jit(solution)/shard_map/while/body/eval_jaxpr/ppermute | solution.py:25
  151.4 9.5 %collective-permute-done = bf16[64,4096]{1,0:T(8,128)(2,1)S(1)} collective-permute-done((bf16[64,4096]{1,0:T(8,128)(2,1)}, bf16[64,4096]{1,0:T(8,128)(2,1)S(1)}, u32[]{:S(2)}, u32[]{:S(2)}) %collective-permute-start) | collective-permute-done | bytes 524320 | tf_op jit(solution)/shard_map/while/body/eval_jaxpr/ppermute | solution.py:25
  165.8 5.3 fusion.167
  177.8 8.5 %collective-permute-done = bf16[64,4096]{1,0:T(8,128)(2,1)S(1)} collective-permute-done((bf16[64,4096]{1,0:T(8,128)(2,1)}, bf16[64,4096]{1,0:T(8,128)(2,1)S(1)}, u32[]{:S(2)}, u32[]{:S(2)}) %collective-permute-start) | collective-permute-done | bytes 524320 | tf_op jit(solution)/shard_map/while/body/eval_jaxpr/ppermute | solution.py:25
  191.2 21.2 %collective-permute-done.4 = bf16[2,64,4096]{2,1,0:T(8,128)(2,1)S(1)} collective-permute-done((bf16[2,64,4096]{2,1,0:T(8,128)(2,1)}, bf16[2,64,4096]{2,1,0:T(8,128)(2,1)S(1)}, u32[]{:S(2)}, u32[]{:S(2)}) %collective-permute-start.4) | collective-permute-done | bytes 1048608 | tf_op jit(solution)/shard_map/ppermute | solution.py:19
  214.2 20.3 %collective-permute-done.5 = bf16[2,64,4096]{2,1,0:T(8,128)(2,1)} collective-permute-done((bf16[2,64,4096]{2,1,0:T(8,128)(2,1)S(1)}, bf16[2,64,4096]{2,1,0:T(8,128)(2,1)}, u32[]{:S(2)}, u32[]{:S(2)}) %collective-permute-start.5) | collective-permute-done | bytes 1048608 | tf_op jit(solution)/shard_map/ppermute | solution.py:19
  234.6 88.6 %while.100 = (s32[]{:T(128)}, bf16[64,4096]{1,0:T(8,128)(2,1)S(1)}, bf16[2,64,4096]{2,1,0:T(8,128)(2,1)S(1)}, bf16[2,64,4096]{2,1,0:T(8,128)(2,1)}, pred[]{:T(51...) while((s32[]{:T(128)}, bf16[64,4096]{1,0:T(8,128)(2,1)S(1)}, ...), condition=%wide.region_9.10_spmd, body=%wide.region_5.9_spmd.sunk | while | flops 543330368 | bytes 33600432 | solution.py:128
  239.7 5.3 fusion.174
  249.0 6.1 collective-permute-done.1
  260.1 5.3 fusion.174
  272.2 5.3 collective-permute-done.1
  294.6 5.3 collective-permute-done.1
  305.0 5.3 fusion.174
  317.9 5.3 collective-permute-done.1
  326.5 96.1 %while.102 = (s32[]{:T(128)}, bf16[64,4096]{1,0:T(8,128)(2,1)S(1)}, bf16[2,64,4096]{2,1,0:T(8,128)(2,1)}, bf16[2,64,4096]{2,1,0:T(8,128)(2,1)}, bf16[2,64,512]{2...) while((s32[]{:T(128)}, bf16[64,4096]{1,0:T(8,128)(2,1)S(1)}, ...), condition=%wide.region_16.17_spmd.clone, body=%wide.region_10.16_spmd.clone.sunk | while | flops 815870080 | bytes 96502704 | solution.py:183
  345.9 11.0 %collective-permute-done.3 = bf16[64,4096]{1,0:T(8,128)(2,1)S(1)} collective-permute-done((bf16[64,4096]{1,0:T(8,128)(2,1)S(1)}, bf16[64,4096]{1,0:T(8,128)(2,1)S(1)}, u32[]{:S(2)}, u32[]{:S(2)}) %collective-permute-start.3) | collective-permute-done | bytes 524320 | tf_op jit(solution)/shard_map/while/body/eval_jaxpr/ppermute | solution.py:25
  376.1 11.0 %collective-permute-done.3 = bf16[64,4096]{1,0:T(8,128)(2,1)S(1)} collective-permute-done((bf16[64,4096]{1,0:T(8,128)(2,1)S(1)}, bf16[64,4096]{1,0:T(8,128)(2,1)S(1)}, u32[]{:S(2)}, u32[]{:S(2)}) %collective-permute-start.3) | collective-permute-done | bytes 524320 | tf_op jit(solution)/shard_map/while/body/eval_jaxpr/ppermute | solution.py:25
  406.3 16.3 %collective-permute-done.3 = bf16[64,4096]{1,0:T(8,128)(2,1)S(1)} collective-permute-done((bf16[64,4096]{1,0:T(8,128)(2,1)S(1)}, bf16[64,4096]{1,0:T(8,128)(2,1)S(1)}, u32[]{:S(2)}, u32[]{:S(2)}) %collective-permute-start.3) | collective-permute-done | bytes 524320 | tf_op jit(solution)/shard_map/while/body/eval_jaxpr/ppermute | solution.py:25
  425.2 13.0 %collective-permute-done.6 = bf16[2,64,4096]{2,1,0:T(8,128)(2,1)S(1)} collective-permute-done((bf16[2,64,4096]{2,1,0:T(8,128)(2,1)}, bf16[2,64,4096]{2,1,0:T(8,128)(2,1)S(1)}, u32[]{:S(2)}, u32[]{:S(2)}) %collective-permute-start.6) | collective-permute-done | bytes 1048608 | tf_op jit(solution)/shard_map/ppermute | solution.py:19
  439.3 13.8 %collective-permute-done.7 = bf16[2,64,4096]{2,1,0:T(8,128)(2,1)} collective-permute-done((bf16[2,64,4096]{2,1,0:T(8,128)(2,1)S(1)}, bf16[2,64,4096]{2,1,0:T(8,128)(2,1)}, u32[]{:S(2)}, u32[]{:S(2)}) %collective-permute-start.7) | collective-permute-done | bytes 1048608 | tf_op jit(solution)/shard_map/ppermute | solution.py:19
  453.1 125.1 %while.101 = (s32[]{:T(128)}, bf16[64,4096]{1,0:T(8,128)(2,1)S(1)}, bf16[2,64,4096]{2,1,0:T(8,128)(2,1)}, bf16[2,64,4096]{2,1,0:T(8,128)(2,1)}, bf16[2,64,512]{2...) while((s32[]{:T(128)}, bf16[64,4096]{1,0:T(8,128)(2,1)S(1)}, ...), condition=%wide.region_23.24_spmd, body=%wide.region_17.23_spmd.sunk | while | flops 816914560 | bytes 94603768 | solution.py:183
  473.9 9.8 %collective-permute-done.2 = bf16[64,4096]{1,0:T(8,128)(2,1)S(1)} collective-permute-done((bf16[64,4096]{1,0:T(8,128)(2,1)S(1)}, bf16[64,4096]{1,0:T(8,128)(2,1)S(1)}, u32[]{:S(2)}, u32[]{:S(2)}) %collective-permute-start.2) | collective-permute-done | bytes 524320 | tf_op jit(solution)/shard_map/while/body/eval_jaxpr/ppermute | solution.py:25
  504.5 10.6 %collective-permute-done.2 = bf16[64,4096]{1,0:T(8,128)(2,1)S(1)} collective-permute-done((bf16[64,4096]{1,0:T(8,128)(2,1)S(1)}, bf16[64,4096]{1,0:T(8,128)(2,1)S(1)}, u32[]{:S(2)}, u32[]{:S(2)}) %collective-permute-start.2) | collective-permute-done | bytes 524320 | tf_op jit(solution)/shard_map/while/body/eval_jaxpr/ppermute | solution.py:25
  536.0 10.7 %collective-permute-done.2 = bf16[64,4096]{1,0:T(8,128)(2,1)S(1)} collective-permute-done((bf16[64,4096]{1,0:T(8,128)(2,1)S(1)}, bf16[64,4096]{1,0:T(8,128)(2,1)S(1)}, u32[]{:S(2)}, u32[]{:S(2)}) %collective-permute-start.2) | collective-permute-done | bytes 524320 | tf_op jit(solution)/shard_map/while/body/eval_jaxpr/ppermute | solution.py:25
  567.5 10.7 %collective-permute-done.2 = bf16[64,4096]{1,0:T(8,128)(2,1)S(1)} collective-permute-done((bf16[64,4096]{1,0:T(8,128)(2,1)S(1)}, bf16[64,4096]{1,0:T(8,128)(2,1)S(1)}, u32[]{:S(2)}, u32[]{:S(2)}) %collective-permute-start.2) | collective-permute-done | bytes 524320 | tf_op jit(solution)/shard_map/while/body/eval_jaxpr/ppermute | solution.py:25
  587.8 32.1 %all-to-all-done.1 = bf16[128,8,512]{2,0,1:T(8,128)(2,1)S(1)} async-done(((bf16[128,8,512]{2,0,1:T(8,128)(2,1)}), bf16[128,8,512]{2,0,1:T(8,128)(2,1)S(1)}, u32[]{:S(2)}, u32[]{:S(2)}) %all-to-all-start.1) | async-done | bytes 1048608 | tf_op jit(solution)/shard_map/all_to_all | solution.py:219
  625.3 48.2 %all-reduce = f32[4096]{0:T(1024)S(1)} all-reduce(f32[4096]{0:T(1024)S(1)} %get-tuple-element.1276), channel_id=2, replica_groups=mesh['section'=4,'dp'=8] {'dp'}, use_global_device_ids=true, to_apply=%region_24.25.clone | all-reduce | flops 4096 | bytes 32768
  (500 shorter events, 266.7 us)
Async XLA Ops:
  7.2 52.3 %all-gather.5.cloned.1.call-start = ((), (), s32[]{:S(2)}) async-start(), calls=%async_computation.2 | async-start | bytes 4718592 | tf_op jit(solution)/shard_map/all_gather | solution.py:88
  7.9 99.1 %all-gather.7.cloned.1.call-start = ((), (), s32[]{:S(2)}) async-start(), calls=%async_computation.3 | async-start | bytes 4718592 | tf_op jit(solution)/shard_map/all_gather | solution.py:89
  119.3 15.3 %collective-permute-start = (bf16[64,4096]{1,0:T(8,128)(2,1)}, bf16[64,4096]{1,0:T(8,128)(2,1)S(1)}, u32[]{:S(2)}, u32[]{:S(2)}) collective-permute-start(bf16[64,4096]{1,0:T(8,128)(2,1)} %get-tuple-element.1834), channel_id=1, source_target_pairs={{0,8},{8,16},{16,24},{1,9},{9,17},{17,25},{2,10},{10,18},{18,26},{... | collective-permute-start | bytes 1572872 | tf_op jit(solution)/shard_map/while/body/eval_jaxpr/ppermute | solution.py:25
  145.5 15.3 %collective-permute-start = (bf16[64,4096]{1,0:T(8,128)(2,1)}, bf16[64,4096]{1,0:T(8,128)(2,1)S(1)}, u32[]{:S(2)}, u32[]{:S(2)}) collective-permute-start(bf16[64,4096]{1,0:T(8,128)(2,1)} %get-tuple-element.1834), channel_id=1, source_target_pairs={{0,8},{8,16},{16,24},{1,9},{9,17},{17,25},{2,10},{10,18},{18,26},{... | collective-permute-start | bytes 1572872 | tf_op jit(solution)/shard_map/while/body/eval_jaxpr/ppermute | solution.py:25
  171.9 14.4 %collective-permute-start = (bf16[64,4096]{1,0:T(8,128)(2,1)}, bf16[64,4096]{1,0:T(8,128)(2,1)S(1)}, u32[]{:S(2)}, u32[]{:S(2)}) collective-permute-start(bf16[64,4096]{1,0:T(8,128)(2,1)} %get-tuple-element.1834), channel_id=1, source_target_pairs={{0,8},{8,16},{16,24},{1,9},{9,17},{17,25},{2,10},{10,18},{18,26},{... | collective-permute-start | bytes 1572872 | tf_op jit(solution)/shard_map/while/body/eval_jaxpr/ppermute | solution.py:25
  186.3 26.1 %collective-permute-start.4 = (bf16[2,64,4096]{2,1,0:T(8,128)(2,1)}, bf16[2,64,4096]{2,1,0:T(8,128)(2,1)S(1)}, u32[]{:S(2)}, u32[]{:S(2)}) collective-permute-start(bf16[2,64,4096]{2,1,0:T(8,128)(2,1)} %get-tuple-element.1974), channel_id=1, source_target_pairs={{0,8},{8,0},{16,24},{24,16},{1,9},{9,1},{17,25},{25,17},{2,10},{10... | collective-permute-start | bytes 3145736 | tf_op jit(solution)/shard_map/ppermute | solution.py:19
  212.4 22.2 %collective-permute-start.5 = (bf16[2,64,4096]{2,1,0:T(8,128)(2,1)S(1)}, bf16[2,64,4096]{2,1,0:T(8,128)(2,1)}, u32[]{:S(2)}, u32[]{:S(2)}) collective-permute-start(bf16[2,64,4096]{2,1,0:T(8,128)(2,1)S(1)} %collective-permute-done.4), channel_id=1, source_target_pairs={{0,16},{16,0},{8,24},{24,8},{1,17},{17,1},{9,25},{25,9},{2,18},{18... | collective-permute-start | bytes 3145736 | tf_op jit(solution)/shard_map/ppermute | solution.py:19
  245.8 9.3 %collective-permute-start.1 = (bf16[64,4096]{1,0:T(8,128)(2,1)}, bf16[64,4096]{1,0:T(8,128)(2,1)S(1)}, u32[]{:S(2)}, u32[]{:S(2)}) collective-permute-start(bf16[64,4096]{1,0:T(8,128)(2,1)} %get-tuple-element.1850), channel_id=1, source_target_pairs={{0,8},{8,16},{16,24},{1,9},{9,17},{17,25},{2,10},{10,18},{18,26},{... | collective-permute-start | bytes 1572872 | tf_op jit(solution)/shard_map/while/body/eval_jaxpr/ppermute | solution.py:25
  266.3 11.3 %collective-permute-start.1 = (bf16[64,4096]{1,0:T(8,128)(2,1)}, bf16[64,4096]{1,0:T(8,128)(2,1)S(1)}, u32[]{:S(2)}, u32[]{:S(2)}) collective-permute-start(bf16[64,4096]{1,0:T(8,128)(2,1)} %get-tuple-element.1850), channel_id=1, source_target_pairs={{0,8},{8,16},{16,24},{1,9},{9,17},{17,25},{2,10},{10,18},{18,26},{... | collective-permute-start | bytes 1572872 | tf_op jit(solution)/shard_map/while/body/eval_jaxpr/ppermute | solution.py:25
  288.7 11.3 %collective-permute-start.1 = (bf16[64,4096]{1,0:T(8,128)(2,1)}, bf16[64,4096]{1,0:T(8,128)(2,1)S(1)}, u32[]{:S(2)}, u32[]{:S(2)}) collective-permute-start(bf16[64,4096]{1,0:T(8,128)(2,1)} %get-tuple-element.1850), channel_id=1, source_target_pairs={{0,8},{8,16},{16,24},{1,9},{9,17},{17,25},{2,10},{10,18},{18,26},{... | collective-permute-start | bytes 1572872 | tf_op jit(solution)/shard_map/while/body/eval_jaxpr/ppermute | solution.py:25
  311.1 12.1 %collective-permute-start.1 = (bf16[64,4096]{1,0:T(8,128)(2,1)}, bf16[64,4096]{1,0:T(8,128)(2,1)S(1)}, u32[]{:S(2)}, u32[]{:S(2)}) collective-permute-start(bf16[64,4096]{1,0:T(8,128)(2,1)} %get-tuple-element.1850), channel_id=1, source_target_pairs={{0,8},{8,16},{16,24},{1,9},{9,17},{17,25},{2,10},{10,18},{18,26},{... | collective-permute-start | bytes 1572872 | tf_op jit(solution)/shard_map/while/body/eval_jaxpr/ppermute | solution.py:25
  343.6 13.3 %copy-start.12 = (bf16[2,64,4096]{2,1,0:T(8,128)(2,1)}, bf16[2,64,4096]{2,1,0:T(8,128)(2,1)S(1)}, u32[]{:S(2)}) copy-start(bf16[2,64,4096]{2,1,0:T(8,128)(2,1)S(1)} %get-tuple-element.2074) | copy-start | bytes 3145732 | tf_op jit(solution)/shard_map/while
  344.6 12.3 %collective-permute-start.3 = (bf16[64,4096]{1,0:T(8,128)(2,1)S(1)}, bf16[64,4096]{1,0:T(8,128)(2,1)S(1)}, u32[]{:S(2)}, u32[]{:S(2)}) collective-permute-start(bf16[64,4096]{1,0:T(8,128)(2,1)S(1)} %bitcast_select_fusion.33), channel_id=1, source_target_pairs={{8,0},{16,8},{24,16},{9,1},{17,9},{25,17},{10,2},{18,10},{26,18},{... | collective-permute-start | bytes 1572872 | tf_op jit(solution)/shard_map/while/body/eval_jaxpr/ppermute | solution.py:25
  373.8 13.3 %copy-start.12 = (bf16[2,64,4096]{2,1,0:T(8,128)(2,1)}, bf16[2,64,4096]{2,1,0:T(8,128)(2,1)S(1)}, u32[]{:S(2)}) copy-start(bf16[2,64,4096]{2,1,0:T(8,128)(2,1)S(1)} %get-tuple-element.2074) | copy-start | bytes 3145732 | tf_op jit(solution)/shard_map/while
  374.8 12.3 %collective-permute-start.3 = (bf16[64,4096]{1,0:T(8,128)(2,1)S(1)}, bf16[64,4096]{1,0:T(8,128)(2,1)S(1)}, u32[]{:S(2)}, u32[]{:S(2)}) collective-permute-start(bf16[64,4096]{1,0:T(8,128)(2,1)S(1)} %bitcast_select_fusion.33), channel_id=1, source_target_pairs={{8,0},{16,8},{24,16},{9,1},{17,9},{25,17},{10,2},{18,10},{26,18},{... | collective-permute-start | bytes 1572872 | tf_op jit(solution)/shard_map/while/body/eval_jaxpr/ppermute | solution.py:25
  404.0 18.6 %copy-start.12 = (bf16[2,64,4096]{2,1,0:T(8,128)(2,1)}, bf16[2,64,4096]{2,1,0:T(8,128)(2,1)S(1)}, u32[]{:S(2)}) copy-start(bf16[2,64,4096]{2,1,0:T(8,128)(2,1)S(1)} %get-tuple-element.2074) | copy-start | bytes 3145732 | tf_op jit(solution)/shard_map/while
  404.9 17.6 %collective-permute-start.3 = (bf16[64,4096]{1,0:T(8,128)(2,1)S(1)}, bf16[64,4096]{1,0:T(8,128)(2,1)S(1)}, u32[]{:S(2)}, u32[]{:S(2)}) collective-permute-start(bf16[64,4096]{1,0:T(8,128)(2,1)S(1)} %bitcast_select_fusion.33), channel_id=1, source_target_pairs={{8,0},{16,8},{24,16},{9,1},{17,9},{25,17},{10,2},{18,10},{26,18},{... | collective-permute-start | bytes 1572872 | tf_op jit(solution)/shard_map/while/body/eval_jaxpr/ppermute | solution.py:25
  422.6 15.6 %collective-permute-start.6 = (bf16[2,64,4096]{2,1,0:T(8,128)(2,1)}, bf16[2,64,4096]{2,1,0:T(8,128)(2,1)S(1)}, u32[]{:S(2)}, u32[]{:S(2)}) collective-permute-start(bf16[2,64,4096]{2,1,0:T(8,128)(2,1)} %get-tuple-element.2096), channel_id=1, source_target_pairs={{0,8},{8,0},{16,24},{24,16},{1,9},{9,1},{17,25},{25,17},{2,10},{10... | collective-permute-start | bytes 3145736 | tf_op jit(solution)/shard_map/ppermute | solution.py:19
  438.1 14.9 %collective-permute-start.7 = (bf16[2,64,4096]{2,1,0:T(8,128)(2,1)S(1)}, bf16[2,64,4096]{2,1,0:T(8,128)(2,1)}, u32[]{:S(2)}, u32[]{:S(2)}) collective-permute-start(bf16[2,64,4096]{2,1,0:T(8,128)(2,1)S(1)} %collective-permute-done.6), channel_id=1, source_target_pairs={{0,16},{16,0},{8,24},{24,8},{1,17},{17,1},{9,25},{25,9},{2,18},{18... | collective-permute-start | bytes 3145736 | tf_op jit(solution)/shard_map/ppermute | solution.py:19
  470.1 13.6 %copy-start.26 = (bf16[4096]{0:T(1024)(128)(2,1)S(1)}, bf16[4096]{0:T(1024)(128)(2,1)}, u32[]{:S(2)}) copy-start(bf16[4096]{0:T(1024)(128)(2,1)} %copy-done.25) | copy-start | bytes 24580 | tf_op jit(solution)/shard_map/while
  472.6 11.1 %collective-permute-start.2 = (bf16[64,4096]{1,0:T(8,128)(2,1)S(1)}, bf16[64,4096]{1,0:T(8,128)(2,1)S(1)}, u32[]{:S(2)}, u32[]{:S(2)}) collective-permute-start(bf16[64,4096]{1,0:T(8,128)(2,1)S(1)} %bitcast_select_fusion.32), channel_id=1, source_target_pairs={{8,0},{16,8},{24,16},{9,1},{17,9},{25,17},{10,2},{18,10},{26,18},{... | collective-permute-start | bytes 1572872 | tf_op jit(solution)/shard_map/while/body/eval_jaxpr/ppermute | solution.py:25
  500.7 14.5 %copy-start.26 = (bf16[4096]{0:T(1024)(128)(2,1)S(1)}, bf16[4096]{0:T(1024)(128)(2,1)}, u32[]{:S(2)}) copy-start(bf16[4096]{0:T(1024)(128)(2,1)} %copy-done.25) | copy-start | bytes 24580 | tf_op jit(solution)/shard_map/while
  503.2 12.0 %collective-permute-start.2 = (bf16[64,4096]{1,0:T(8,128)(2,1)S(1)}, bf16[64,4096]{1,0:T(8,128)(2,1)S(1)}, u32[]{:S(2)}, u32[]{:S(2)}) collective-permute-start(bf16[64,4096]{1,0:T(8,128)(2,1)S(1)} %bitcast_select_fusion.32), channel_id=1, source_target_pairs={{8,0},{16,8},{24,16},{9,1},{17,9},{25,17},{10,2},{18,10},{26,18},{... | collective-permute-start | bytes 1572872 | tf_op jit(solution)/shard_map/while/body/eval_jaxpr/ppermute | solution.py:25
  532.2 14.5 %copy-start.26 = (bf16[4096]{0:T(1024)(128)(2,1)S(1)}, bf16[4096]{0:T(1024)(128)(2,1)}, u32[]{:S(2)}) copy-start(bf16[4096]{0:T(1024)(128)(2,1)} %copy-done.25) | copy-start | bytes 24580 | tf_op jit(solution)/shard_map/while
  534.7 12.0 %collective-permute-start.2 = (bf16[64,4096]{1,0:T(8,128)(2,1)S(1)}, bf16[64,4096]{1,0:T(8,128)(2,1)S(1)}, u32[]{:S(2)}, u32[]{:S(2)}) collective-permute-start(bf16[64,4096]{1,0:T(8,128)(2,1)S(1)} %bitcast_select_fusion.32), channel_id=1, source_target_pairs={{8,0},{16,8},{24,16},{9,1},{17,9},{25,17},{10,2},{18,10},{26,18},{... | collective-permute-start | bytes 1572872 | tf_op jit(solution)/shard_map/while/body/eval_jaxpr/ppermute | solution.py:25
  563.7 14.5 %copy-start.26 = (bf16[4096]{0:T(1024)(128)(2,1)S(1)}, bf16[4096]{0:T(1024)(128)(2,1)}, u32[]{:S(2)}) copy-start(bf16[4096]{0:T(1024)(128)(2,1)} %copy-done.25) | copy-start | bytes 24580 | tf_op jit(solution)/shard_map/while
  566.2 12.0 %collective-permute-start.2 = (bf16[64,4096]{1,0:T(8,128)(2,1)S(1)}, bf16[64,4096]{1,0:T(8,128)(2,1)S(1)}, u32[]{:S(2)}, u32[]{:S(2)}) collective-permute-start(bf16[64,4096]{1,0:T(8,128)(2,1)S(1)} %bitcast_select_fusion.32), channel_id=1, source_target_pairs={{8,0},{16,8},{24,16},{9,1},{17,9},{25,17},{10,2},{18,10},{26,18},{... | collective-permute-start | bytes 1572872 | tf_op jit(solution)/shard_map/while/body/eval_jaxpr/ppermute | solution.py:25
  581.2 42.8 %copy-start.33 = (u32[32]{0:T(128)S(1)}, u32[32]{0:T(128)}, u32[]{:S(2)}) copy-start(u32[32]{0:T(128)} %constant.780) | copy-start | bytes 388
  581.2 38.6 %all-to-all-start.1 = ((bf16[128,8,512]{2,0,1:T(8,128)(2,1)}), bf16[128,8,512]{2,0,1:T(8,128)(2,1)S(1)}, u32[]{:S(2)}, u32[]{:S(2)}) async-start(bf16[128,8,512]{2,0,1:T(8,128)(2,1)} %copy.13), calls=%async_computation.1 | async-start | bytes 2097152 | tf_op jit(solution)/shard_map/all_to_all | solution.py:219
  584.9 89.2 %all-gather.11.cloned.1.call-start = ((), (), s32[]{:S(2)}) async-start(), calls=%async_computation.5 | async-start | bytes 1179648 | tf_op jit(solution)/shard_map/all_gather | solution.py:224
  619.9 57.8 %all-to-all-start = ((bf16[128,8,512]{0,2,1:T(8,128)(2,1)}), bf16[128,8,512]{0,2,1:T(8,128)(2,1)S(1)}, u32[]{:S(2)}, u32[]{:S(2)}) async-start(bf16[128,8,512]{0,2,1:T(8,128)(2,1)} %copy.12), calls=%async_computation | async-start | bytes 2097152 | tf_op jit(solution)/shard_map/all_to_all | solution.py:218
  623.4 54.2 %all-gather.9.cloned.1.call-start = ((), (), s32[]{:S(2)}) async-start(), calls=%async_computation.4 | async-start | bytes 1179648 | tf_op jit(solution)/shard_map/all_gather | solution.py:223
  (103 other events, 452.9 us)
Sparse Core Ops, SparseCore 0:
  9.6 49.8 all-gather.4
  61.1 45.8 all-gather.6
  587.4 33.4 all-gather.10
  625.6 33.7 all-gather.8
where the time goes:
time: 689 us; the launch traced here: 688 us
  waiting for transfers between devices  317 us (46%)
  matrix products  96.7 us (14%)
  other arithmetic  95.1 us (14%)
  blocking collectives  62.7 us (9%)
  starting transfers between devices  54.1 us (8%)
  local copies, waits for them, and re-layouts  44.6 us (6%)
  between operations  14.6 us (2%)
    ppermute x14, waiting for transfers between devices, from_behind(): return lax.ppermute(block, axis, route)  130 us
    ppermute x4, waiting for transfers between devices, from_partner(): return lax.ppermute(block, axis, route)  68.2 us
    unnamed x1, blocking collectives  48.2 us
    all_gather x1, waiting for transfers between devices, body(): lax.all_gather(w_restore, 'dp', axis=2, tiled=True)  47.5 us
    dot_general x7, matrix products, section_forward(): jnp.dot(active, matrix_restore, preferred_element_type=jnp.float32)  36.8 us
    all_gather x1, waiting for transfers between devices, body(): lax.all_gather(w_reduce, 'dp', axis=1, tiled=True)  36.2 us
    ppermute x14, starting transfers between devices, from_behind(): return lax.ppermute(block, axis, route)  36.2 us
    all_to_all x1, waiting for transfers between devices, body(): lax.all_to_all(upstream_all, 'dp', split_axis=1, concat_axis=0, tiled=True)  32.1 us
  transfers between devices with their start and end apart: 24, of which 21 were waited for; matrix products, arithmetic and copies ran while one was open for 3% of the time, Pallas kernels for 0%

commit v1 on v0

v1 whole, which is shorter than its diff:
```python
import functools

import jax
import jax.numpy as jnp
from jax import lax
from jax.experimental import pallas as pl
from jax.experimental.pallas import tpu as pltpu
from jax.sharding import PartitionSpec as P

POOL = 4
EPSILON = 1e-06
EXTRA = 128
HALF = 64
F32 = jnp.float32
BF16 = jnp.bfloat16


def dot(a, b, ca, cb):
    return lax.dot_general(a, b, (((ca,), (cb,)), ((), ())), preferred_element_type=F32)


def split_lanes(column, rows):
    high = column.astype(BF16).astype(F32)
    low = column - high
    lane = lax.broadcasted_iota(jnp.int32, (rows, EXTRA), 1)
    return jnp.where(lane < HALF, high, low).astype(BF16)


def joined(block, R):
    return block[:, R : R + 1] + block[:, R + HALF : R + HALF + 1]


def kernel(
    S, N, D, frames, grad_out, gain, gain_col, w_reduce, w_restore,
    out_gain, out_reduce, out_restore,
    xs, gs, wr, wt, gains, ns, acts, all_n, all_a, all_g, all_u,
    psend, pland, pfull, qsend, qland, ufull, pmine,
    local_sem, in_send, in_recv, w_send, w_recv, p_send, p_recv, q_send, q_recv,
    o_send, o_recv,
):
    me_s, me_d = lax.axis_index("section"), lax.axis_index("dp")
    T, F = xs.shape[1], xs.shape[2]
    R = w_reduce.shape[1]
    B = T // N
    middle = S // 2
    peers = [lax.rem(me_d + i, N) for i in range(1, N)]
    others = [lax.rem(me_s + i, S) for i in range(1, S)]
    sends = []

    def rows(k, size=B):
        return pl.ds(pl.multiple_of(k * size, size), size)

    def remote(src, dst, send, recv, **device):
        return pltpu.make_async_remote_copy(
            src_ref=src, dst_ref=dst, send_sem=send, recv_sem=recv,
            device_id=device, device_id_type=pl.DeviceIdType.MESH,
        )

    barrier = pltpu.get_barrier_semaphore()
    for k in peers:
        pl.semaphore_signal(barrier, inc=1, device_id={"dp": k}, device_id_type=pl.DeviceIdType.MESH)
    for t in others:
        pl.semaphore_signal(barrier, inc=1, device_id={"section": t}, device_id_type=pl.DeviceIdType.MESH)

    mine = rows(me_d)

    def cols(k):
        return pl.ds(pl.multiple_of(k * F, F), F)

    local = [
        pltpu.make_async_copy(frames.at[rows(me_s), cols(me_d)], xs.at[0, mine], local_sem.at[0]),
        pltpu.make_async_copy(grad_out.at[rows(me_s), cols(me_d)], gs.at[S - 1, mine], local_sem.at[1]),
        pltpu.make_async_copy(w_reduce, wr.at[me_s], local_sem.at[2]),
        pltpu.make_async_copy(w_restore, wt.at[me_s], local_sem.at[3]),
        pltpu.make_async_copy(gain, gains.at[me_s], local_sem.at[4]),
    ]
    for c in local:
        c.start()
    pl.semaphore_wait(barrier, N - 1 + S - 1)

    def weights(which, src, dst, i):
        t = others[i]
        return remote(src, dst.at[me_s], w_send.at[which, i], w_recv.at[which, me_s], section=t)

    frame_copies = [
        remote(frames.at[rows(me_s), cols(k)], xs.at[0, mine], in_send.at[0, i], in_recv.at[0, i], dp=k)
        for i, k in enumerate(peers)
    ]
    for c in frame_copies:
        c.start()
    for i in range(S - 1):
        for which, src, dst in ((0, gain, gains), (1, w_reduce, wr)):
            c = weights(which, src, dst, i)
            c.start()
            sends.append(c)
    for i in range(S - 1):
        c = weights(2, w_restore, wt, i)
        c.start()
        sends.append(c)
    grad_copies = [
        remote(grad_out.at[rows(me_s), cols(k)], gs.at[S - 1, mine], in_send.at[1, i], in_recv.at[1, i], dp=k)
        for i, k in enumerate(peers)
    ]
    for c in grad_copies:
        c.start()
    sends += frame_copies + grad_copies
    for c in local:
        c.wait()
    for c in frame_copies:
        c.wait_recv()

    def weights_here(which, t):
        src, dst = ((gain, gains), (w_reduce, wr), (w_restore, wt))[which]

        @pl.when(me_s != t)
        def _():
            remote(src, dst.at[t], w_send.at[which, 0], w_recv.at[which, t], section=others[0]).wait_recv()

    def scatter(sent, land, send, recv):
        copies = [remote(sent.at[rows(k)], land.at[me_d], send.at[i], recv.at[i], dp=k) for i, k in enumerate(peers)]
        for c in copies:
            c.start()
        land[me_d] = sent[mine]
        sends.extend(copies)
        return copies

    def total(copies, land):
        for c in copies:
            c.wait_recv()
        result = land[0].astype(F32)
        for k in range(1, N):
            result += land[k].astype(F32)
        return result

    def share(full, send, recv):
        copies = [remote(full.at[mine], full.at[mine], send.at[i], recv.at[i], dp=k) for i, k in enumerate(peers)]
        for c in copies:
            c.start()
        sends.extend(copies)
        return copies

    owed = []

    def to_owner(which, src, dst, t):
        spot = rows(me_s, T)

        def copy():
            return remote(src, dst.at[spot], o_send.at[which, t], o_recv.at[which, me_s], section=t)

        @pl.when(me_s != t)
        def _():
            copy().start()

        @pl.when(me_s == t)
        def _():
            dst[spot] = src[...]

        owed.append((t, copy))

    def pooled(block):
        i = lax.broadcasted_iota(jnp.int32, (T, T), 0) >> (POOL.bit_length() - 1)
        j = lax.broadcasted_iota(jnp.int32, (T, T), 1) >> (POOL.bit_length() - 1)
        return dot(jnp.where(i == j, 1.0 / POOL, 0.0).astype(BF16), block, 1, 0)

    def q_scatter(s):
        qsend[s] = dot(gs[s], wt[s], 1, 1).astype(BF16)
        return scatter(qsend.at[s], qland.at[s], q_send.at[s, 0], q_recv.at[s, 0])

    def u_share(s, copies):
        q = total(copies, qland.at[s])
        p = pmine[s]
        gate = jax.nn.sigmoid(p)
        ufull[s, mine] = (q * gate * (1.0 + p * (1.0 - gate))).astype(BF16)
        return share(ufull.at[s], q_send.at[s, 1], q_recv.at[s, 1])

    skips = []
    early = None
    early_share = None
    for s in range(S):
        weights_here(0, s)
        weights_here(1, s)
        x = xs[s].astype(F32)
        part = dot((x * gains[s, 0:1]).astype(BF16), wr[s], 1, 0)
        psend[s, :, :R] = part.astype(BF16)
        psend[s, :, R:] = split_lanes(jnp.sum(x * x, axis=1, keepdims=True), T)
        copies = scatter(psend.at[s], pland.at[s], p_send.at[s, 0], p_recv.at[s, 0])
        if s == S - 1:
            for c in grad_copies:
                c.wait_recv()
            weights_here(2, s)
            early = q_scatter(s)
        block = total(copies, pland.at[s])
        inverse = lax.rsqrt(joined(block, R) / D + EPSILON)
        before = block[:, :R] * inverse
        pmine[s] = before
        pfull[s, mine, :R] = before.astype(BF16)
        pfull[s, mine, R:] = split_lanes(inverse, B)
        copies = share(pfull.at[s], p_send.at[s, 1], p_recv.at[s, 1])
        if s == S - 1:
            early_share = u_share(s, early)
        for c in copies:
            c.wait_recv()
        full = pfull[s].astype(F32)
        p = full[:, :R]
        acts[s] = (p * jax.nn.sigmoid(p)).astype(BF16)
        if s < S - 1:
            weights_here(2, s)
            x = xs[s].astype(F32)
            y = (x + dot(acts[s], wt[s], 1, 0)).astype(BF16)
            if s + 1 < middle:
                xs[s + 1] = y
            elif s + 1 == middle:
                xs[s + 1] = (pooled(y) + y.astype(F32)).astype(BF16)
            else:
                xs[s + 1] = (y.astype(F32) + skips[S - 2 - s][...].astype(F32)).astype(BF16)
            if s < middle:
                skips.append(xs.at[s + 1])
        ns[s] = (xs[s].astype(F32) * joined(full, R)).astype(BF16)
        to_owner(0, ns.at[s], all_n, s)
        to_owner(1, acts.at[s], all_a, s)

    for s in reversed(range(S)):
        if s == S - 1:
            copies = early_share
        else:
            copies = u_share(s, q_scatter(s))
        to_owner(2, gs.at[s], all_g, s)
        for c in copies:
            c.wait_recv()
        to_owner(3, ufull.at[s], all_u, s)
        if s > 0:
            u = ufull[s]
            full = pfull[s].astype(F32)
            shift = jnp.sum(u.astype(F32) * full[:, :R], axis=1, keepdims=True) / D
            inverse = joined(full, R)
            normal = xs[s].astype(F32) * inverse
            m = dot(u, wr[s], 1, 1) * gains[s, 0:1]
            e = (gs[s].astype(F32) + inverse * (m - normal * shift)).astype(BF16)
            if s - 1 >= middle:
                gs[s - 1] = e
            elif s == middle:
                gs[s - 1] = (pooled(e) + e.astype(F32)).astype(BF16)
            else:
                gs[s - 1] = (e.astype(F32) + gs[S - 1 - s].astype(F32)).astype(BF16)

    def arrived(which, src, dst):
        for i in range(1, S):
            remote(
                src, dst.at[rows(others[i - 1], T)], o_send.at[which, 0], o_recv.at[which, others[i - 1]],
                section=others[i - 1],
            ).wait_recv()

    arrived(1, acts.at[0], all_a)
    arrived(2, gs.at[0], all_g)
    out_restore[...] = dot(all_a[...], all_g[...], 0, 0)
    arrived(0, ns.at[0], all_n)
    arrived(3, ufull.at[0], all_u)
    term = dot(all_n[...], all_u[...], 0, 0)
    out_reduce[...] = term * gain_col[...]
    out_gain[...] = lax.dot_general(
        jnp.ones((8, R), F32), term * wr[me_s].astype(F32), (((1,), (1,)), ((), ())),
        precision=lax.Precision.HIGHEST, preferred_element_type=F32,
    )
    for c in sends:
        c.wait_send()
    for t, copy in owed:

        @pl.when(me_s != t)
        def _(copy=copy):
            copy().wait_send()


def solution(mesh):
    S, N = mesh.shape["section"], mesh.shape["dp"]

    def body(frames, grad_out, norm_gain, w_reduce, w_restore):
        D = frames.shape[2]
        F, R = w_reduce.shape[1], w_reduce.shape[2]
        held = frames.shape[0] * frames.shape[1]
        B = held // S
        T = B * N
        vmem = pl.BlockSpec(memory_space=pltpu.VMEM)
        anywhere = pl.BlockSpec(memory_space=pl.ANY)
        dma = pltpu.SemaphoreType.DMA
        out_gain, out_reduce, out_restore = pl.pallas_call(
            functools.partial(kernel, S, N, D),
            out_shape=(
                jax.ShapeDtypeStruct((8, F), F32),
                jax.ShapeDtypeStruct((F, R), F32),
                jax.ShapeDtypeStruct((R, F), F32),
            ),
            in_specs=[anywhere, anywhere, vmem, vmem, anywhere, anywhere],
            out_specs=(vmem, vmem, vmem),
            scratch_shapes=[
                pltpu.VMEM((S, T, F), BF16),
                pltpu.VMEM((S, T, F), BF16),
                pltpu.VMEM((S, F, R), BF16),
                pltpu.VMEM((S, R, F), BF16),
                pltpu.VMEM((S, 8, F), F32),
                pltpu.VMEM((S, T, F), BF16),
                pltpu.VMEM((S, T, R), BF16),
                pltpu.VMEM((S * T, F), BF16),
                pltpu.VMEM((S * T, R), BF16),
                pltpu.VMEM((S * T, F), BF16),
                pltpu.VMEM((S * T, R), BF16),
                pltpu.VMEM((S, T, R + EXTRA), BF16),
                pltpu.VMEM((S, N, B, R + EXTRA), BF16),
                pltpu.VMEM((S, T, R + EXTRA), BF16),
                pltpu.VMEM((S, T, R), BF16),
                pltpu.VMEM((S, N, B, R), BF16),
                pltpu.VMEM((S, T, R), BF16),
                pltpu.VMEM((S, B, R), F32),
                dma((5,)), dma((2, N - 1)), dma((2, N - 1)), dma((3, S - 1)), dma((3, S)),
                dma((S, 2, N - 1)), dma((S, 2, N - 1)), dma((S, 2, N - 1)), dma((S, 2, N - 1)), dma((4, S)), dma((4, S)),
            ],
            compiler_params=pltpu.CompilerParams(
                collective_id=0, has_side_effects=True, vmem_limit_bytes=50 * 1024 * 1024
            ),
        )(
            frames.reshape(held, D),
            grad_out.reshape(held, D),
            jnp.broadcast_to(norm_gain.astype(F32), (8, F)),
            norm_gain.astype(F32).reshape(F, 1),
            w_reduce[0],
            w_restore[0],
        )
        return out_gain[:1], out_reduce[None], out_restore[None]

    in_specs = (
        P(None, "dp", None),
        P(None, "dp", None),
        P("section", "dp"),
        P("section", "dp", None),
        P("section", None, "dp"),
    )
    out_specs = (P("section", "dp"), P("section", "dp", None), P("section", None, "dp"))
    return jax.shard_map(body, mesh=mesh, in_specs=in_specs, out_specs=out_specs, check_vma=False)
```

time: 689 us -> 187 us (0.27)
  waiting for transfers between devices: 317 us -> 0 us
  Pallas kernels: 0 us -> 181 us
  matrix products: 96.7 us -> 0 us
  other arithmetic: 95.1 us -> 0.01 us
  blocking collectives: 62.7 us -> 0 us
  starting transfers between devices: 54.1 us -> 0 us
  local copies, waits for them, and re-layouts: 44.6 us -> 5.42 us
  between operations: 14.6 us -> 0.67 us
    ppermute x18 -> x0, waiting for transfers between devices: 199 us -> none  [the longest x14 130 us: from_behind(): return lax.ppermute(block, axis, route)]
    pallas_call x0 -> x1, Pallas kernels: none -> 181 us  [body(): pl.pallas_call(functools.partial(kernel, S, N, D), out_shape=(jax.ShapeDt...]
    dot_general x30 -> x0, matrix products: 96.7 us -> none  [the longest x7 36.8 us: section_forward(): jnp.dot(active, matrix_restore, preferred_element_type=jnp.float32)]
    all_gather x4 -> x0, waiting for transfers between devices: 83.8 us -> none  [the longest x1 47.5 us: body(): lax.all_gather(w_restore, 'dp', axis=2, tiled=True)]
    scatter x28 -> x0, other arithmetic: 60.2 us -> none  [the longest x7 22.9 us: backward_advance(): kept_array.at[chosen].set(jnp.where(usable, fresh_item, kept_array[chosen]))]
    unnamed x1 -> x0, blocking collectives: 48.2 us -> none
    ppermute x18 -> x0, starting transfers between devices: 46.7 us -> none  [the longest x14 36.2 us: from_behind(): return lax.ppermute(block, axis, route)]
    all_to_all x2 -> x0, waiting for transfers between devices: 32.1 us -> none  [the longest x1 32.1 us: body(): lax.all_to_all(upstream_all, 'dp', split_axis=1, concat_axis=0, tiled=True)]
  transfers between devices with their start and end apart: 24 -> 0, of which waited for: 21 -> 0; matrix products, arithmetic and copies ran while one was open for 3% -> 0% of each run, Pallas kernels for 0% -> 0%
where the time goes in v1:
time: 187 us
  Pallas kernels  181 us (97%)
  local copies, waits for them, and re-layouts  5.42 us (3%)
    pallas_call x1, Pallas kernels, body(): pl.pallas_call(functools.partial(kernel, S, N, D), out_shape=(jax.ShapeDt...  181 us
    unnamed x8, local copies, waits for them, and re-layouts  4.7 us

profile of v1, /device:TPU:0, one launch (start us, length us, event | category | flops | bytes accessed | tf_op | source)
XLA Modules:
  0.0 186.9 jit_solution(8723898162159468709)
XLA Ops:
  0.6 0.0 copy-start.2
  0.6 0.7 copy-done.2
  1.3 0.1 copy.8.gain_col
  1.5 0.0 copy-start
  1.5 1.0 copy-done
  2.5 0.0 copy-start.1
  2.5 1.0 copy-done.1
  3.6 180.8 %shard_map.76 = (f32[8,512]{1,0:T(8,128)S(1)}, f32[512,512]{1,0:T(8,128)S(1)}, f32[512,512]{1,0:T(8,128)S(1)}) custom-call(bf16[128,4096]{1,0:T(8,128)(2,1)} %bitcast.13, bf16[128,4096]{1,0:T(8,128)(2,1)} %bitcast.14, f32[8,512]{1,0:T(8,128)S(1)} %broadcast_in_dim.14.gain, f32[512,1]{1,0:T(8,128)S(1)} %copy.8.gain_col, bf16[512,512]{1,0:T(8,128)(2,1)S(1)} %bitcast.11, ...), custom_call_target="tpu_custom_call" | custom-call | tf_op jit(solution)/shard_map/pallas_call | solution.py:285
  184.4 0.6 slice.3
  185.0 1.0 copy.11
  185.9 1.0 copy.12
  (2 shorter events, 0.0 us)
Async XLA Ops:
  0.6 0.7 copy-start.2
  1.5 1.0 copy-start
  2.5 1.0 copy-start.1

commit v2 on v1

--- a/solution.py
+++ b/solution.py
@@ -34,7 +34,7 @@
     S, N, D, frames, grad_out, gain, gain_col, w_reduce, w_restore,
     out_gain, out_reduce, out_restore,
     xs, gs, wr, wt, gains, ns, acts, all_n, all_a, all_g, all_u,
-    psend, pland, pfull, qsend, qland, ufull, pmine,
+    psend, ppair, pland, pfull, qsend, qpair, qland, ufull, pmine,
     local_sem, in_send, in_recv, w_send, w_recv, p_send, p_recv, q_send, q_recv,
     o_send, o_recv,
 ):
@@ -62,7 +62,10 @@
     for t in others:
         pl.semaphore_signal(barrier, inc=1, device_id={"section": t}, device_id_type=pl.DeviceIdType.MESH)
 
-    mine = rows(me_d)
+    M = N // 2
+    chip, core = lax.div(me_d, 2), lax.rem(me_d, 2)
+    partner = me_d + 1 - 2 * core
+    mine = rows(core * M + chip)
 
     def cols(k):
         return pl.ds(pl.multiple_of(k * F, F), F)
@@ -116,11 +119,23 @@
         def _():
             remote(src, dst.at[t], w_send.at[which, 0], w_recv.at[which, t], section=others[0]).wait_recv()
 
-    def scatter(sent, land, send, recv):
-        copies = [remote(sent.at[rows(k)], land.at[me_d], send.at[i], recv.at[i], dp=k) for i, k in enumerate(peers)]
-        for c in copies:
+    def scatter(sent, pair, send, recv):
+        c = remote(sent.at[rows(1 - core, T // 2)], pair, send.at[0], recv.at[0], dp=partner)
+        c.start()
+        sends.append(c)
+        return c
+
+    def spread(copy, sent, pair, land, send, recv):
+        copy.wait_recv()
+        own = sent[rows(core, T // 2)].astype(F32)
+        pair[...] = (own + pair[...].astype(F32)).astype(BF16)
+        copies = []
+        for i in range(1, M):
+            place = lax.rem(chip + i, M)
+            c = remote(pair.at[rows(place)], land.at[chip], send.at[i], recv.at[i], dp=2 * place + core)
             c.start()
-        land[me_d] = sent[mine]
+            copies.append(c)
+        land[chip] = pair[rows(chip)]
         sends.extend(copies)
         return copies
 
@@ -128,16 +143,33 @@
         for c in copies:
             c.wait_recv()
         result = land[0].astype(F32)
-        for k in range(1, N):
+        for k in range(1, M):
             result += land[k].astype(F32)
         return result
 
     def share(full, send, recv):
-        copies = [remote(full.at[mine], full.at[mine], send.at[i], recv.at[i], dp=k) for i, k in enumerate(peers)]
-        for c in copies:
+        copies = []
+        for i in range(1, M):
+            place = lax.rem(chip + i, M)
+            copies.append(remote(full.at[mine], full.at[mine], send.at[i], recv.at[i], dp=2 * place + core))
+        passed = []
+        for i in range(M):
+            block = rows(core * M + lax.rem(chip - i + M, M))
+            passed.append(
+                remote(full.at[block], full.at[block], send.at[M + i], recv.at[M + i], dp=partner)
+            )
+        for c in copies + passed[:1]:
             c.start()
-        sends.extend(copies)
-        return copies
+        sends.extend(copies + passed)
+        return copies, passed
+
+    def gather(shared):
+        copies, passed = shared
+        for c, onward in zip(copies, passed[1:]):
+            c.wait_recv()
+            onward.start()
+        for c in passed:
+            c.wait_recv()
 
     owed = []
 
@@ -164,7 +196,10 @@
 
     def q_scatter(s):
         qsend[s] = dot(gs[s], wt[s], 1, 1).astype(BF16)
-        return scatter(qsend.at[s], qland.at[s], q_send.at[s, 0], q_recv.at[s, 0])
+        return scatter(qsend.at[s], qpair.at[s], q_send.at[s, 0], q_recv.at[s, 0])
+
+    def q_spread(s, copy):
+        return spread(copy, qsend.at[s], qpair.at[s], qland.at[s], q_send.at[s, 0], q_recv.at[s, 0])
 
     def u_share(s, copies):
         q = total(copies, qland.at[s])
@@ -183,12 +218,15 @@
         part = dot((x * gains[s, 0:1]).astype(BF16), wr[s], 1, 0)
         psend[s, :, :R] = part.astype(BF16)
         psend[s, :, R:] = split_lanes(jnp.sum(x * x, axis=1, keepdims=True), T)
-        copies = scatter(psend.at[s], pland.at[s], p_send.at[s, 0], p_recv.at[s, 0])
+        copies = scatter(psend.at[s], ppair.at[s], p_send.at[s, 0], p_recv.at[s, 0])
         if s == S - 1:
             for c in grad_copies:
                 c.wait_recv()
             weights_here(2, s)
             early = q_scatter(s)
+        copies = spread(copies, psend.at[s], ppair.at[s], pland.at[s], p_send.at[s, 0], p_recv.at[s, 0])
+        if s == S - 1:
+            early = q_spread(s, early)
         block = total(copies, pland.at[s])
         inverse = lax.rsqrt(joined(block, R) / D + EPSILON)
         before = block[:, :R] * inverse
@@ -198,8 +236,7 @@
         copies = share(pfull.at[s], p_send.at[s, 1], p_recv.at[s, 1])
         if s == S - 1:
             early_share = u_share(s, early)
-        for c in copies:
-            c.wait_recv()
+        gather(copies)
         full = pfull[s].astype(F32)
         p = full[:, :R]
         acts[s] = (p * jax.nn.sigmoid(p)).astype(BF16)
@@ -223,10 +260,9 @@
         if s == S - 1:
             copies = early_share
         else:
-            copies = u_share(s, q_scatter(s))
+            copies = u_share(s, q_spread(s, q_scatter(s)))
         to_owner(2, gs.at[s], all_g, s)
-        for c in copies:
-            c.wait_recv()
+        gather(copies)
         to_owner(3, ufull.at[s], all_u, s)
         if s > 0:
             u = ufull[s]
@@ -304,14 +340,16 @@
                 pltpu.VMEM((S * T, F), BF16),
                 pltpu.VMEM((S * T, R), BF16),
                 pltpu.VMEM((S, T, R + EXTRA), BF16),
-                pltpu.VMEM((S, N, B, R + EXTRA), BF16),
+                pltpu.VMEM((S, T // 2, R + EXTRA), BF16),
+                pltpu.VMEM((S, N // 2, B, R + EXTRA), BF16),
                 pltpu.VMEM((S, T, R + EXTRA), BF16),
                 pltpu.VMEM((S, T, R), BF16),
-                pltpu.VMEM((S, N, B, R), BF16),
+                pltpu.VMEM((S, T // 2, R), BF16),
+                pltpu.VMEM((S, N // 2, B, R), BF16),
                 pltpu.VMEM((S, T, R), BF16),
                 pltpu.VMEM((S, B, R), F32),
                 dma((5,)), dma((2, N - 1)), dma((2, N - 1)), dma((3, S - 1)), dma((3, S)),
-                dma((S, 2, N - 1)), dma((S, 2, N - 1)), dma((S, 2, N - 1)), dma((S, 2, N - 1)), dma((4, S)), dma((4, S)),
+                dma((S, 2, N)), dma((S, 2, N)), dma((S, 2, N)), dma((S, 2, N)), dma((4, S)), dma((4, S)),
             ],
             compiler_params=pltpu.CompilerParams(
                 collective_id=0, has_side_effects=True, vmem_limit_bytes=50 * 1024 * 1024

time: 187 us -> 159 us (0.85)
  Pallas kernels: 181 us -> 152 us
    pallas_call x1, Pallas kernels: 181 us -> 152 us  [body(): pl.pallas_call(functools.partial(kernel, S, N, D), out_shape=(jax.ShapeDt...]
where the time goes in v2:
time: 159 us; the launch traced here: 158 us
  Pallas kernels  152 us (96%)
  local copies, waits for them, and re-layouts  5.42 us (3%)
    pallas_call x1, Pallas kernels, body(): pl.pallas_call(functools.partial(kernel, S, N, D), out_shape=(jax.ShapeDt...  152 us
    unnamed x8, local copies, waits for them, and re-layouts  4.7 us

profile of v2, /device:TPU:0, one launch (start us, length us, event | category | flops | bytes accessed | tf_op | source)
XLA Modules:
  0.0 158.4 jit_solution(1783495459929833043)
XLA Ops:
  0.6 0.0 copy-start.2
  0.6 0.7 copy-done.2
  1.3 0.1 copy.8.gain_col
  1.5 0.0 copy-start
  1.5 1.0 copy-done
  2.5 0.0 copy-start.1
  2.5 1.0 copy-done.1
  3.6 152.3 %shard_map.76 = (f32[8,512]{1,0:T(8,128)S(1)}, f32[512,512]{1,0:T(8,128)S(1)}, f32[512,512]{1,0:T(8,128)S(1)}) custom-call(bf16[128,4096]{1,0:T(8,128)(2,1)} %bitcast.13, bf16[128,4096]{1,0:T(8,128)(2,1)} %bitcast.14, f32[8,512]{1,0:T(8,128)S(1)} %broadcast_in_dim.14.gain, f32[512,1]{1,0:T(8,128)S(1)} %copy.8.gain_col, bf16[512,512]{1,0:T(8,128)(2,1)S(1)} %bitcast.11, ...), custom_call_target="tpu_custom_call" | custom-call | tf_op jit(solution)/shard_map/pallas_call | solution.py:321
  155.9 0.6 slice.3
  156.5 1.0 copy.11
  157.4 1.0 copy.12
  (2 shorter events, 0.0 us)
Async XLA Ops:
  0.6 0.7 copy-start.2
  1.5 1.0 copy-start
  2.5 1.0 copy-start.1

commit v3 on v2

--- a/solution.py
+++ b/solution.py
@@ -91,15 +91,12 @@
     ]
     for c in frame_copies:
         c.start()
+    first_sends = []
     for i in range(S - 1):
         for which, src, dst in ((0, gain, gains), (1, w_reduce, wr)):
             c = weights(which, src, dst, i)
             c.start()
-            sends.append(c)
-    for i in range(S - 1):
-        c = weights(2, w_restore, wt, i)
-        c.start()
-        sends.append(c)
+            first_sends.append(c)
     grad_copies = [
         remote(grad_out.at[rows(me_s), cols(k)], gs.at[S - 1, mine], in_send.at[1, i], in_recv.at[1, i], dp=k)
         for i, k in enumerate(peers)
@@ -109,6 +106,12 @@
     sends += frame_copies + grad_copies
     for c in local:
         c.wait()
+    for c in first_sends:
+        c.wait_send()
+    for i in range(S - 1):
+        c = weights(2, w_restore, wt, i)
+        c.start()
+        sends.append(c)
     for c in frame_copies:
         c.wait_recv()
 
@@ -208,6 +211,11 @@
         ufull[s, mine] = (q * gate * (1.0 + p * (1.0 - gate))).astype(BF16)
         return share(ufull.at[s], q_send.at[s, 1], q_recv.at[s, 1])
 
+    def keep(s):
+        ns[s] = (xs[s].astype(F32) * joined(pfull[s].astype(F32), R)).astype(BF16)
+        to_owner(0, ns.at[s], all_n, s)
+        to_owner(1, acts.at[s], all_a, s)
+
     skips = []
     early = None
     early_share = None
@@ -219,6 +227,8 @@
         psend[s, :, :R] = part.astype(BF16)
         psend[s, :, R:] = split_lanes(jnp.sum(x * x, axis=1, keepdims=True), T)
         copies = scatter(psend.at[s], ppair.at[s], p_send.at[s, 0], p_recv.at[s, 0])
+        if s > 0:
+            keep(s - 1)
         if s == S - 1:
             for c in grad_copies:
                 c.wait_recv()
@@ -252,16 +262,17 @@
                 xs[s + 1] = (y.astype(F32) + skips[S - 2 - s][...].astype(F32)).astype(BF16)
             if s < middle:
                 skips.append(xs.at[s + 1])
-        ns[s] = (xs[s].astype(F32) * joined(full, R)).astype(BF16)
-        to_owner(0, ns.at[s], all_n, s)
-        to_owner(1, acts.at[s], all_a, s)
 
     for s in reversed(range(S)):
         if s == S - 1:
             copies = early_share
         else:
-            copies = u_share(s, q_spread(s, q_scatter(s)))
-        to_owner(2, gs.at[s], all_g, s)
+            copies = q_scatter(s)
+            to_owner(2, gs.at[s], all_g, s)
+            if s == S - 2:
+                keep(S - 1)
+                to_owner(2, gs.at[S - 1], all_g, S - 1)
+            copies = u_share(s, q_spread(s, copies))
         gather(copies)
         to_owner(3, ufull.at[s], all_u, s)
         if s > 0:

time: 159 us -> 155 us (0.975)
  Pallas kernels: 152 us -> 148 us
    pallas_call x1, Pallas kernels: 152 us -> 148 us  [body(): pl.pallas_call(functools.partial(kernel, S, N, D), out_shape=(jax.ShapeDt...]
where the time goes in v3:
time: 155 us; the launch traced here: 154 us
  Pallas kernels  148 us (95%)
  local copies, waits for them, and re-layouts  5.42 us (3%)
    pallas_call x1, Pallas kernels, body(): pl.pallas_call(functools.partial(kernel, S, N, D), out_shape=(jax.ShapeDt...  148 us
    unnamed x8, local copies, waits for them, and re-layouts  4.7 us

profile of v3, /device:TPU:0, one launch (start us, length us, event | category | flops | bytes accessed | tf_op | source)
XLA Modules:
  0.0 154.5 jit_solution(18279751574677795202)
XLA Ops:
  0.6 0.0 copy-start.2
  0.6 0.7 copy-done.2
  1.3 0.1 copy.8.gain_col
  1.5 0.0 copy-start
  1.5 1.0 copy-done
  2.5 0.0 copy-start.1
  2.5 1.0 copy-done.1
  3.6 148.4 %shard_map.76 = (f32[8,512]{1,0:T(8,128)S(1)}, f32[512,512]{1,0:T(8,128)S(1)}, f32[512,512]{1,0:T(8,128)S(1)}) custom-call(bf16[128,4096]{1,0:T(8,128)(2,1)} %bitcast.13, bf16[128,4096]{1,0:T(8,128)(2,1)} %bitcast.14, f32[8,512]{1,0:T(8,128)S(1)} %broadcast_in_dim.14.gain, f32[512,1]{1,0:T(8,128)S(1)} %copy.8.gain_col, bf16[512,512]{1,0:T(8,128)(2,1)S(1)} %bitcast.11, ...), custom_call_target="tpu_custom_call" | custom-call | tf_op jit(solution)/shard_map/pallas_call | solution.py:332
  152.0 0.6 slice.3
  152.6 1.0 copy.11
  153.5 1.0 copy.12
  (2 shorter events, 0.0 us)
Async XLA Ops:
  0.6 0.7 copy-start.2
  1.5 1.0 copy-start
  2.5 1.0 copy-start.1
